TPU v7x, 512 devices: a whole 4x4x16 slice. The times are simulated.
512 devices in a mesh: recv: 128 (over z, x, core), src: 4 (over y).
Axes of the slice: x: 4, y: 4, z: 16, core: 2. Of those that a mesh axis runs over, the one named last changes fastest.
Arguments:
- interactions: int32 [3, 49152], P(None, ('recv', 'src')), may hold values from 0 to 4095, as said below
- list_lengths: int32 [512], P(('recv', 'src')), may hold values from 48 to 96, as said below
- kernels: float32 [2048, 128, 16, 128], P(('recv', 'src')), may hold values from -0.0210316469 to 0.0210316469
- prestress: float32 [4096, 128], P(('recv', 'src')), may hold values from 2 to 3
- friction: float32 [4096, 128], P(('recv', 'src')), may hold values from 0.2 to 0.5
- load_rate: float32 [4096, 128], P(('recv', 'src')), may hold values from 0.04 to 0.08
Outputs:
- slip_rates: float32 [4096, 96, 128], P(('recv', 'src'))
Inputs may be any that keep to these rules, and one draw needn't show every extreme that they name: `interactions`: column e belongs to device block g = e // 96, g = i * 4 + j. Its receiver patch lies in [i * 4 * 8, (i + 1) * 4 * 8); its source patch p satisfies (p // 8) mod 4 == j; its owner is p // 32; its lag offset lies in [32, 48]. The entries of one block name at most 1 distinct source patches of one owner, and in every draw some owner supplies exactly that many distinct source patches to every block. `list_lengths`: some device's list is full and some device's list holds exactly half, in every draw.
All inputs are finite; a program needn't handle non-finite values.
Results may differ from a plain program's by a relative error of at most 0.0003.
Values sent between devices are 32-bit elements; how exact they have to be, the bound alone decides.
A program may use at most 128 MiB of HBM per device.

v0:
```python
import jax
import jax.numpy as jnp
from jax import lax
from jax.sharding import PartitionSpec as P

BLOCK = 32
BLOCKS = 3
NEWTON = 4
damping = 0.5


def inverse_sinh(values):
    magnitude = jnp.abs(values)
    result = jnp.log(magnitude + jnp.sqrt(1.0 + magnitude * magnitude))
    return jnp.where(values < 0, -result, result)


def friction_solve(drive, friction):
    rates = jnp.zeros_like(drive)
    for newton_step in range(NEWTON):
        misfit = damping * rates + friction * inverse_sinh(rates) - drive
        slope_now = damping + friction * lax.rsqrt(1.0 + rates * rates)
        rates = rates - misfit / slope_now
    return rates


def local(interactions, list_lengths, kernels, prestress, friction, load_rate):
    n_recv = lax.axis_size("recv")
    n_src = lax.axis_size("src")
    recv_idx = lax.axis_index("recv")
    src_idx = lax.axis_index("src")
    ent_count = interactions.shape[1]
    ker_count = kernels.shape[0]
    width = kernels.shape[1]
    lag_count = kernels.shape[2]
    patch_count = prestress.shape[0]
    per_kernel = ent_count // ker_count
    peer_cap = max(1, ent_count // (8 * n_recv))
    group_rows = n_src * patch_count
    receivers = interactions[0] - recv_idx * group_rows
    sources = interactions[1]
    owners = sources // group_rows
    local_patch = sources % patch_count
    delays = interactions[2]
    entry_numbers = jnp.arange(ent_count, dtype=jnp.int32)
    same_source = sources[None, :] == sources[:, None]
    first_of = jnp.min(jnp.where(same_source, entry_numbers[None, :], ent_count), axis=1)
    is_first = first_of == entry_numbers
    earlier = (
        (owners[None, :] == owners[:, None])
        & is_first[None, :]
        & (entry_numbers[None, :] < first_of[:, None])
    )
    ranks = jnp.sum(earlier.astype(jnp.int32), axis=1)
    slot_of = owners * peer_cap + ranks
    slot_ids = jnp.arange(n_recv * peer_cap, dtype=jnp.int32)
    filling = (slot_ids[:, None] == slot_of[None, :]) & is_first[None, :]
    wanted = jnp.sum(jnp.where(filling, local_patch[None, :], 0), axis=1)
    asked = lax.all_to_all(
        wanted.reshape(n_recv, peer_cap), "recv", split_axis=0, concat_axis=0, tiled=True
    ).reshape(-1)
    live = (entry_numbers < list_lengths[0]).astype(jnp.float32)
    patch_ids = jnp.arange(group_rows, dtype=jnp.int32)
    route_table = jnp.where(patch_ids[:, None] == receivers[None, :], live[None, :], 0.0)
    kernel_matrices = kernels.reshape(ker_count, width, lag_count * width)

    def cut_window(window, delay):
        return lax.dynamic_slice_in_dim(
            window, 2 * BLOCK - delay - (lag_count - 1), BLOCK + lag_count - 1, 0
        )

    def one_kernel(pair):
        segs, kern = pair
        pieces = [
            segs[:, lag_count - 1 - lag_idx : lag_count - 1 - lag_idx + BLOCK]
            for lag_idx in range(lag_count)
        ]
        stacked_rows = jnp.stack(pieces, axis=2).reshape(per_kernel * BLOCK, lag_count * width)
        return jnp.einsum("mk,rk->mr", stacked_rows, kern, precision=lax.Precision.HIGHEST)

    finished_blocks = []
    for block_idx in range(BLOCKS):
        if block_idx == 0:
            stress = jnp.zeros((patch_count, BLOCK, width), jnp.float32)
        else:
            recent = jnp.concatenate(finished_blocks[max(0, block_idx - 2) :], axis=1)
            span = recent.shape[1]
            outgoing = jnp.take(recent, asked, axis=0).reshape(n_recv, peer_cap, span, width)
            received = lax.all_to_all(outgoing, "recv", split_axis=0, concat_axis=0, tiled=True)
            picked = jnp.take(received.reshape(n_recv * peer_cap, span, width), slot_of, axis=0)
            windows = jnp.pad(picked, ((0, 0), (2 * BLOCK - span, 0), (0, 0)))
            segments = jax.vmap(cut_window)(windows, delays)
            grouped = segments.reshape(ker_count, per_kernel, BLOCK + lag_count - 1, width)
            stress_terms = lax.map(one_kernel, (grouped, kernel_matrices)).reshape(
                ent_count, BLOCK * width
            )
            summed = jnp.dot(route_table, stress_terms, precision=lax.Precision.HIGHEST)
            partial_terms = summed.reshape(group_rows, BLOCK, width)
            summed_all = lax.psum(partial_terms, "src")
            stress = lax.dynamic_slice_in_dim(summed_all, src_idx * patch_count, patch_count, 0)
        times = (block_idx * BLOCK + 1 + jnp.arange(BLOCK, dtype=jnp.int32)).astype(jnp.float32)
        drive = prestress[:, None, :] + load_rate[:, None, :] * times[None, :, None] + stress
        finished_blocks.append(friction_solve(drive, friction[:, None, :]))
    return jnp.concatenate(finished_blocks, axis=1)


def solution(mesh):
    in_specs = (
        P(None, ("recv", "src")),
        P(("recv", "src")),
        P(("recv", "src"), None, None, None),
        P(("recv", "src"), None),
        P(("recv", "src"), None),
        P(("recv", "src"), None),
    )
    out_specs = P(("recv", "src"), None, None)
    return jax.shard_map(local, mesh=mesh, in_specs=in_specs, out_specs=out_specs, check_vma=False)
```

profile of v0, /device:TPU:2, one launch (start us, length us, event | category | flops | bytes accessed | tf_op | source)
XLA Modules:
  0.0 748.2 jit_solution(15495887555175844307)
XLA Ops:
  9.3 19.4 %all-to-all-start = ((s32[128,1,1]{2,1,0:T(1,128)}), s32[128,1,1]{2,1,0:T(1,128)S(1)}, u32[]{:S(2)}, u32[]{:S(2)}) async-start(s32[128,1,1]{2,1,0:T(1,128)} %copy.163), calls=%async_computation | async-start | bytes 131072 | tf_op jit(solution)/shard_map/all_to_all | solution.py:59
  30.6 11.9 %all-to-all-done = s32[128,1,1]{2,1,0:T(1,128)S(1)} async-done(((s32[128,1,1]{2,1,0:T(1,128)}), s32[128,1,1]{2,1,0:T(1,128)S(1)}, u32[]{:S(2)}, u32[]{:S(2)}) %all-to-all-start) | async-done | bytes 544 | tf_op jit(solution)/shard_map/all_to_all | solution.py:59
  60.6 89.8 %all-to-all-done.1 = f32[128,1,32,128]{3,2,1,0:T(8,128)S(1)} async-done(((f32[128,1,32,128]{3,2,1,0:T(8,128)}), f32[128,1,32,128]{3,2,1,0:T(8,128)S(1)}, u32[]{:S(2)}, u32[]{:S(2)}) %all-to-all-start.1) | async-done | bytes 2097184 | tf_op jit(solution)/shard_map/all_to_all | solution.py:89
  165.0 117.7 %while.20 = (s32[]{:T(128)}, f32[4,768,128]{2,1,0:T(8,128)}, f32[4,24,47,128]{3,1,0,2:T(8,128)}, f32[4,128,2048]{2,1,0:T(8,128)}, s32[]{:T(128)}) while((s32[]{:T(128)}, f32[4,768,128]{2,1,0:T(8,128)}, f32[4,24,47,128]{3,1,0,2:T(8,128)}, f32[4,128,2048]{2,1,0:T(8,128)}, s32[]{:T(128)}) %tuple.92), condition=%wide.region_4.5_spmd, body=%wide.region_3.4_spmd.sunk | while | flops 2415919104 | bytes 35210304 | solution.py:94
  168.7 16.2 %stack.104 = f32[24,32,16,128]{3,2,1,0:T(8,128)} concatenate(f32[24,32,1,128]{3,2,1,0:T(1,128)} %bitcast.321, f32[24,32,1,128]{3,2,1,0:T(1,128)} %bitcast.320, f32[24,32,1,128]{3,2,1,0:T(1,128)} %bitcast.319, f32[24,32,1,128]{3,2,1,0:T(1,128)} %bitcast.318, f32[24,32,1,128]{3,2,1,0:T(1,128)} %bitcast.317, f32[24,32,1,128]{3,2,1,0:T(1,128)} %bitcast.316, ...), dimensions={2} | concatenate | bytes 12582912 | tf_op jit(solution)/shard_map/while/body/eval_jaxpr/stack | solution.py:78
  184.9 9.9 %fusion.111 = f32[4,768,128]{2,1,0:T(8,128)} fusion(f32[4,768,128]{2,1,0:T(8,128)} %get-tuple-element.267, s32[]{:T(128)} %get-tuple-element.266, f32[96,8,16,128]{3,2,1,0:T(8,128)} %bitcast.304, f32[4,128,2048]{2,1,0:T(8,128)} %get-tuple-element.274), kind=kOutput, calls=%fused_computation.10.clone.1 | convolution fusion | flops 2415919104 | bytes 7734272 | tf_op jit(solution)/shard_map/while/body/eval_jaxpr/mk,rk->mr/dot_general | solution.py:79
  198.0 16.2 %stack.104 = f32[24,32,16,128]{3,2,1,0:T(8,128)} concatenate(f32[24,32,1,128]{3,2,1,0:T(1,128)} %bitcast.321, f32[24,32,1,128]{3,2,1,0:T(1,128)} %bitcast.320, f32[24,32,1,128]{3,2,1,0:T(1,128)} %bitcast.319, f32[24,32,1,128]{3,2,1,0:T(1,128)} %bitcast.318, f32[24,32,1,128]{3,2,1,0:T(1,128)} %bitcast.317, f32[24,32,1,128]{3,2,1,0:T(1,128)} %bitcast.316, ...), dimensions={2} | concatenate | bytes 12582912 | tf_op jit(solution)/shard_map/while/body/eval_jaxpr/stack | solution.py:78
  214.2 9.9 %fusion.111 = f32[4,768,128]{2,1,0:T(8,128)} fusion(f32[4,768,128]{2,1,0:T(8,128)} %get-tuple-element.267, s32[]{:T(128)} %get-tuple-element.266, f32[96,8,16,128]{3,2,1,0:T(8,128)} %bitcast.304, f32[4,128,2048]{2,1,0:T(8,128)} %get-tuple-element.274), kind=kOutput, calls=%fused_computation.10.clone.1 | convolution fusion | flops 2415919104 | bytes 7734272 | tf_op jit(solution)/shard_map/while/body/eval_jaxpr/mk,rk->mr/dot_general | solution.py:79
  227.3 16.2 %stack.104 = f32[24,32,16,128]{3,2,1,0:T(8,128)} concatenate(f32[24,32,1,128]{3,2,1,0:T(1,128)} %bitcast.321, f32[24,32,1,128]{3,2,1,0:T(1,128)} %bitcast.320, f32[24,32,1,128]{3,2,1,0:T(1,128)} %bitcast.319, f32[24,32,1,128]{3,2,1,0:T(1,128)} %bitcast.318, f32[24,32,1,128]{3,2,1,0:T(1,128)} %bitcast.317, f32[24,32,1,128]{3,2,1,0:T(1,128)} %bitcast.316, ...), dimensions={2} | concatenate | bytes 12582912 | tf_op jit(solution)/shard_map/while/body/eval_jaxpr/stack | solution.py:78
  243.5 9.9 %fusion.111 = f32[4,768,128]{2,1,0:T(8,128)} fusion(f32[4,768,128]{2,1,0:T(8,128)} %get-tuple-element.267, s32[]{:T(128)} %get-tuple-element.266, f32[96,8,16,128]{3,2,1,0:T(8,128)} %bitcast.304, f32[4,128,2048]{2,1,0:T(8,128)} %get-tuple-element.274), kind=kOutput, calls=%fused_computation.10.clone.1 | convolution fusion | flops 2415919104 | bytes 7734272 | tf_op jit(solution)/shard_map/while/body/eval_jaxpr/mk,rk->mr/dot_general | solution.py:79
  256.5 16.2 %stack.104 = f32[24,32,16,128]{3,2,1,0:T(8,128)} concatenate(f32[24,32,1,128]{3,2,1,0:T(1,128)} %bitcast.321, f32[24,32,1,128]{3,2,1,0:T(1,128)} %bitcast.320, f32[24,32,1,128]{3,2,1,0:T(1,128)} %bitcast.319, f32[24,32,1,128]{3,2,1,0:T(1,128)} %bitcast.318, f32[24,32,1,128]{3,2,1,0:T(1,128)} %bitcast.317, f32[24,32,1,128]{3,2,1,0:T(1,128)} %bitcast.316, ...), dimensions={2} | concatenate | bytes 12582912 | tf_op jit(solution)/shard_map/while/body/eval_jaxpr/stack | solution.py:78
  272.8 9.9 %fusion.111 = f32[4,768,128]{2,1,0:T(8,128)} fusion(f32[4,768,128]{2,1,0:T(8,128)} %get-tuple-element.267, s32[]{:T(128)} %get-tuple-element.266, f32[96,8,16,128]{3,2,1,0:T(8,128)} %bitcast.304, f32[4,128,2048]{2,1,0:T(8,128)} %get-tuple-element.274), kind=kOutput, calls=%fused_computation.10.clone.1 | convolution fusion | flops 2415919104 | bytes 7734272 | tf_op jit(solution)/shard_map/while/body/eval_jaxpr/mk,rk->mr/dot_general | solution.py:79
  286.1 54.1 %all-reduce.5.cloned.1.call-done = f32[32,32,128]{2,0,1:T(8,128)} async-done(((f32[32,32,128]{2,0,1:T(8,128)}), f32[32,32,128]{2,0,1:T(8,128)}) %all-reduce.5.cloned.1.call-update) | async-done | bytes 524304 | tf_op jit(solution)/shard_map/psum | solution.py:99
  347.0 201.0 %all_to_all.25 = f32[128,1,64,128]{3,2,1,0:T(8,128)} all-to-all(f32[128,1,64,128]{3,2,1,0:T(8,128)S(1)} %fusion.24), channel_id=1, replica_groups=mesh['recv'=128,'src'=4] {'recv'}, dimensions={0} | all-to-all | bytes 8388608 | tf_op jit(solution)/shard_map/all_to_all | solution.py:89
  562.8 117.4 %while.21 = (s32[]{:T(128)}, f32[4,768,128]{2,1,0:T(8,128)}, f32[4,24,47,128]{3,1,0,2:T(8,128)}, f32[4,128,2048]{2,1,0:T(8,128)}, s32[]{:T(128)}) while((s32[]{:T(128)}, f32[4,768,128]{2,1,0:T(8,128)}, f32[4,24,47,128]{3,1,0,2:T(8,128)}, f32[4,128,2048]{2,1,0:T(8,128)}, s32[]{:T(128)}) %tuple.91), condition=%wide.region_7.8_spmd, body=%wide.region_6.7_spmd.sunk | while | flops 2415919104 | bytes 35210304 | solution.py:94
  566.2 16.2 %stack.105 = f32[24,32,16,128]{3,2,1,0:T(8,128)} concatenate(f32[24,32,1,128]{3,2,1,0:T(1,128)} %bitcast.337, f32[24,32,1,128]{3,2,1,0:T(1,128)} %bitcast.336, f32[24,32,1,128]{3,2,1,0:T(1,128)} %bitcast.335, f32[24,32,1,128]{3,2,1,0:T(1,128)} %bitcast.334, f32[24,32,1,128]{3,2,1,0:T(1,128)} %bitcast.333, f32[24,32,1,128]{3,2,1,0:T(1,128)} %bitcast.332, ...), dimensions={2} | concatenate | bytes 12582912 | tf_op jit(solution)/shard_map/while/body/eval_jaxpr/stack | solution.py:78
  582.4 9.9 %fusion.115 = f32[4,768,128]{2,1,0:T(8,128)} fusion(f32[4,768,128]{2,1,0:T(8,128)} %get-tuple-element.282, s32[]{:T(128)} %get-tuple-element.281, f32[96,8,16,128]{3,2,1,0:T(8,128)} %bitcast.305, f32[4,128,2048]{2,1,0:T(8,128)} %get-tuple-element.289), kind=kOutput, calls=%fused_computation.20.clone.1 | convolution fusion | flops 2415919104 | bytes 7734272 | tf_op jit(solution)/shard_map/while/body/eval_jaxpr/mk,rk->mr/dot_general | solution.py:79
  595.5 16.2 %stack.105 = f32[24,32,16,128]{3,2,1,0:T(8,128)} concatenate(f32[24,32,1,128]{3,2,1,0:T(1,128)} %bitcast.337, f32[24,32,1,128]{3,2,1,0:T(1,128)} %bitcast.336, f32[24,32,1,128]{3,2,1,0:T(1,128)} %bitcast.335, f32[24,32,1,128]{3,2,1,0:T(1,128)} %bitcast.334, f32[24,32,1,128]{3,2,1,0:T(1,128)} %bitcast.333, f32[24,32,1,128]{3,2,1,0:T(1,128)} %bitcast.332, ...), dimensions={2} | concatenate | bytes 12582912 | tf_op jit(solution)/shard_map/while/body/eval_jaxpr/stack | solution.py:78
  611.7 9.9 %fusion.115 = f32[4,768,128]{2,1,0:T(8,128)} fusion(f32[4,768,128]{2,1,0:T(8,128)} %get-tuple-element.282, s32[]{:T(128)} %get-tuple-element.281, f32[96,8,16,128]{3,2,1,0:T(8,128)} %bitcast.305, f32[4,128,2048]{2,1,0:T(8,128)} %get-tuple-element.289), kind=kOutput, calls=%fused_computation.20.clone.1 | convolution fusion | flops 2415919104 | bytes 7734272 | tf_op jit(solution)/shard_map/while/body/eval_jaxpr/mk,rk->mr/dot_general | solution.py:79
  624.8 16.2 %stack.105 = f32[24,32,16,128]{3,2,1,0:T(8,128)} concatenate(f32[24,32,1,128]{3,2,1,0:T(1,128)} %bitcast.337, f32[24,32,1,128]{3,2,1,0:T(1,128)} %bitcast.336, f32[24,32,1,128]{3,2,1,0:T(1,128)} %bitcast.335, f32[24,32,1,128]{3,2,1,0:T(1,128)} %bitcast.334, f32[24,32,1,128]{3,2,1,0:T(1,128)} %bitcast.333, f32[24,32,1,128]{3,2,1,0:T(1,128)} %bitcast.332, ...), dimensions={2} | concatenate | bytes 12582912 | tf_op jit(solution)/shard_map/while/body/eval_jaxpr/stack | solution.py:78
  641.0 9.9 %fusion.115 = f32[4,768,128]{2,1,0:T(8,128)} fusion(f32[4,768,128]{2,1,0:T(8,128)} %get-tuple-element.282, s32[]{:T(128)} %get-tuple-element.281, f32[96,8,16,128]{3,2,1,0:T(8,128)} %bitcast.305, f32[4,128,2048]{2,1,0:T(8,128)} %get-tuple-element.289), kind=kOutput, calls=%fused_computation.20.clone.1 | convolution fusion | flops 2415919104 | bytes 7734272 | tf_op jit(solution)/shard_map/while/body/eval_jaxpr/mk,rk->mr/dot_general | solution.py:79
  654.1 16.2 %stack.105 = f32[24,32,16,128]{3,2,1,0:T(8,128)} concatenate(f32[24,32,1,128]{3,2,1,0:T(1,128)} %bitcast.337, f32[24,32,1,128]{3,2,1,0:T(1,128)} %bitcast.336, f32[24,32,1,128]{3,2,1,0:T(1,128)} %bitcast.335, f32[24,32,1,128]{3,2,1,0:T(1,128)} %bitcast.334, f32[24,32,1,128]{3,2,1,0:T(1,128)} %bitcast.333, f32[24,32,1,128]{3,2,1,0:T(1,128)} %bitcast.332, ...), dimensions={2} | concatenate | bytes 12582912 | tf_op jit(solution)/shard_map/while/body/eval_jaxpr/stack | solution.py:78
  670.3 9.9 %fusion.115 = f32[4,768,128]{2,1,0:T(8,128)} fusion(f32[4,768,128]{2,1,0:T(8,128)} %get-tuple-element.282, s32[]{:T(128)} %get-tuple-element.281, f32[96,8,16,128]{3,2,1,0:T(8,128)} %bitcast.305, f32[4,128,2048]{2,1,0:T(8,128)} %get-tuple-element.289), kind=kOutput, calls=%fused_computation.20.clone.1 | convolution fusion | flops 2415919104 | bytes 7734272 | tf_op jit(solution)/shard_map/while/body/eval_jaxpr/mk,rk->mr/dot_general | solution.py:79
  683.5 55.3 %all-reduce.7.cloned.1.call-done = f32[32,32,128]{2,0,1:T(8,128)} async-done(((f32[32,32,128]{2,0,1:T(8,128)}), f32[32,32,128]{2,0,1:T(8,128)}) %all-reduce.7.cloned.1.call-update) | async-done | bytes 524304 | tf_op jit(solution)/shard_map/psum | solution.py:99
  (125 shorter events, 91.9 us)
Async XLA Ops:
  9.3 33.3 %all-to-all-start = ((s32[128,1,1]{2,1,0:T(1,128)}), s32[128,1,1]{2,1,0:T(1,128)S(1)}, u32[]{:S(2)}, u32[]{:S(2)}) async-start(s32[128,1,1]{2,1,0:T(1,128)} %copy.163), calls=%async_computation | async-start | bytes 131072 | tf_op jit(solution)/shard_map/all_to_all | solution.py:59
  29.4 15.5 %copy-start.7 = (f32[8,128]{1,0:T(8,128)}, f32[8,128]{1,0:T(8,128)S(1)}, u32[]{:S(2)}) copy-start(f32[8,128]{1,0:T(8,128)S(1)} %get-tuple-element.139) | copy-start | bytes 12292
  29.4 15.5 %copy-start.10 = (f32[8,128]{1,0:T(8,128)}, f32[8,128]{1,0:T(8,128)S(1)}, u32[]{:S(2)}) copy-start(f32[8,128]{1,0:T(8,128)S(1)} %get-tuple-element.140) | copy-start | bytes 12292
  30.6 14.4 %copy-start = (f32[8,32,128]{2,0,1:T(8,128)}, f32[8,32,128]{2,0,1:T(8,128)S(1)}, u32[]{:S(2)}) copy-start(f32[8,32,128]{2,0,1:T(8,128)S(1)} %fusion.46) | copy-start | bytes 393220
  47.3 103.2 %all-to-all-start.1 = ((f32[128,1,32,128]{3,2,1,0:T(8,128)}), f32[128,1,32,128]{3,2,1,0:T(8,128)S(1)}, u32[]{:S(2)}, u32[]{:S(2)}) async-start(f32[128,1,32,128]{3,2,1,0:T(8,128)} %fusion.25), calls=%async_computation.1 | async-start | bytes 4194304 | tf_op jit(solution)/shard_map/all_to_all | solution.py:89
  54.0 286.2 %all-reduce.5.cloned.1.call-start = ((), (), s32[]{:S(2)}) async-start(), calls=%async_computation.3 | async-start | bytes 1048576 | tf_op jit(solution)/shard_map/psum | solution.py:99
  54.3 6.2 copy-start.15
  60.6 93.3 %copy-start.16 = (pred[96]{0:T(512)(128)(4,1)}, pred[96]{0:T(512)(128)(4,1)S(1)}, u32[]{:S(2)}) copy-start(pred[96]{0:T(512)(128)(4,1)S(1)} %compare_and_fusion.1) | copy-start | bytes 292
  282.7 57.5 %copy-start.5 = (f32[8,128]{1,0:T(8,128)S(1)}, f32[8,128]{1,0:T(8,128)}, u32[]{:S(2)}) copy-start(f32[8,128]{1,0:T(8,128)} %param.14) | copy-start | bytes 12292
  282.7 57.5 %copy-start.8 = (f32[8,128]{1,0:T(8,128)S(1)}, f32[8,128]{1,0:T(8,128)}, u32[]{:S(2)}) copy-start(f32[8,128]{1,0:T(8,128)} %copy-done.7) | copy-start | bytes 12292
  282.7 57.5 %copy-start.11 = (f32[8,128]{1,0:T(8,128)S(1)}, f32[8,128]{1,0:T(8,128)}, u32[]{:S(2)}) copy-start(f32[8,128]{1,0:T(8,128)} %copy-done.10) | copy-start | bytes 12292
  282.7 57.5 %copy-start.20 = (f32[8,128]{1,0:T(8,128)S(1)}, f32[8,128]{1,0:T(8,128)}, u32[]{:S(2)}) copy-start(f32[8,128]{1,0:T(8,128)} %param.15) | copy-start | bytes 12292
  282.7 57.5 %copy-start.22 = (f32[8,128]{1,0:T(8,128)S(1)}, f32[8,128]{1,0:T(8,128)}, u32[]{:S(2)}) copy-start(f32[8,128]{1,0:T(8,128)} %param.13) | copy-start | bytes 12292
  284.3 57.3 %copy-start.1 = (f32[8,32,128]{2,0,1:T(8,128)S(1)}, f32[8,32,128]{2,0,1:T(8,128)}, u32[]{:S(2)}) copy-start(f32[8,32,128]{2,0,1:T(8,128)} %copy-done) | copy-start | bytes 393220
  286.0 452.8 %all-reduce.7.cloned.1.call-start = ((), (), s32[]{:S(2)}) async-start(), calls=%async_computation.4 | async-start | bytes 1048576 | tf_op jit(solution)/shard_map/psum | solution.py:99
  341.6 2.9 copy-start.3
  548.0 2.9 copy-start.17
  680.2 58.6 %copy-start.6 = (f32[8,128]{1,0:T(8,128)S(1)}, f32[8,128]{1,0:T(8,128)}, u32[]{:S(2)}) copy-start(f32[8,128]{1,0:T(8,128)} %param.14) | copy-start | bytes 12292
  680.2 58.6 %copy-start.9 = (f32[8,128]{1,0:T(8,128)S(1)}, f32[8,128]{1,0:T(8,128)}, u32[]{:S(2)}) copy-start(f32[8,128]{1,0:T(8,128)} %copy-done.7) | copy-start | bytes 12292
  680.2 58.6 %copy-start.12 = (f32[8,128]{1,0:T(8,128)S(1)}, f32[8,128]{1,0:T(8,128)}, u32[]{:S(2)}) copy-start(f32[8,128]{1,0:T(8,128)} %copy-done.10) | copy-start | bytes 12292
  680.2 58.6 %copy-start.21 = (f32[8,128]{1,0:T(8,128)S(1)}, f32[8,128]{1,0:T(8,128)}, u32[]{:S(2)}) copy-start(f32[8,128]{1,0:T(8,128)} %param.15) | copy-start | bytes 12292
  680.2 58.6 %copy-start.23 = (f32[8,128]{1,0:T(8,128)S(1)}, f32[8,128]{1,0:T(8,128)}, u32[]{:S(2)}) copy-start(f32[8,128]{1,0:T(8,128)} %param.13) | copy-start | bytes 12292
  681.8 58.4 %copy-start.2 = (f32[8,32,128]{2,0,1:T(8,128)S(1)}, f32[8,32,128]{2,0,1:T(8,128)}, u32[]{:S(2)}) copy-start(f32[8,32,128]{2,0,1:T(8,128)} %copy-done) | copy-start | bytes 393220
  681.8 58.4 %copy-start.4 = (f32[8,32,128]{2,0,1:T(8,128)S(1)}, f32[8,32,128]{2,0,1:T(8,128)}, u32[]{:S(2)}) copy-start(f32[8,32,128]{2,0,1:T(8,128)} %copy-done.3) | copy-start | bytes 393220
  (4 other events, 8.4 us)
Sparse Core Ops, SparseCore 0:
  286.1 54.0 all-reduce.4
  683.7 55.1 all-reduce.6
where the time goes:
time: 761 us; the launch traced here: 748 us
  waiting for transfers between devices  211 us (28%)
  blocking collectives  201 us (26%)
  local copies, waits for them, and re-layouts  196 us (26%)
  matrix products  82.8 us (11%)
  starting transfers between devices  26.5 us (3%)
  other arithmetic  15.5 us (2%)
  between operations  14.7 us (2%)
    all_to_all x1, blocking collectives, local(): lax.all_to_all(outgoing, 'recv', split_axis=0, concat_axis=0, tiled=True)  201 us
    another operation x8, local copies, waits for them, and re-layouts, one_kernel(): jnp.stack(pieces, axis=2).reshape(per_kernel * BLOCK, lag_count * width)  130 us
    psum x2, waiting for transfers between devices, local(): summed_all = lax.psum(partial_terms, 'src')  109 us
    all_to_all x1, waiting for transfers between devices, local(): lax.all_to_all(outgoing, 'recv', split_axis=0, concat_axis=0, tiled=True)  89.8 us
    dot_general x8, matrix products, one_kernel(): jnp.einsum('mk,rk->mr', stacked_rows, kern, precision=lax.Precision.HIGHEST)  79.5 us
    all_to_all x1, starting transfers between devices, local(): lax.all_to_all(wanted.reshape(n_recv, peer_cap), 'recv', split_axis=0, co...  19.4 us
    gather x2, local copies, waits for them, and re-layouts, cut_window(): lax.dynamic_slice_in_dim(window, 2 * BLOCK - delay - (lag_count - 1), BLO...  17 us
    slice x8, local copies, waits for them, and re-layouts, one_kernel(): segs[:, lag_count - 1 - lag_idx:lag_count - 1 - lag_idx + BLOCK]  15.4 us
  transfers between devices with their start and end apart: 4, of which 4 were waited for; matrix products, arithmetic and copies ran while one was open for 1% of the time, Pallas kernels for 0%

commit v1 on v0

--- a/solution.py
+++ b/solution.py
@@ -96,7 +96,11 @@
             )
             summed = jnp.dot(route_table, stress_terms, precision=lax.Precision.HIGHEST)
             partial_terms = summed.reshape(group_rows, BLOCK, width)
-            summed_all = lax.psum(partial_terms, "src")
+            summed_all = partial_terms
+            for hop in (1, 2):
+                summed_all = summed_all + lax.ppermute(
+                    summed_all, "src", [(dev, dev ^ hop) for dev in range(4)]
+                )
             stress = lax.dynamic_slice_in_dim(summed_all, src_idx * patch_count, patch_count, 0)
         times = (block_idx * BLOCK + 1 + jnp.arange(BLOCK, dtype=jnp.int32)).astype(jnp.float32)
         drive = prestress[:, None, :] + load_rate[:, None, :] * times[None, :, None] + stress

time: 761 us -> 697 us (0.916)
  the two profiles are of different devices: /device:TPU:2 before, /device:TPU:94 now
where the time goes in v1:
time: 697 us; the launch traced here: 683 us
  blocking collectives  197 us (28%)
  local copies, waits for them, and re-layouts  195 us (28%)
  waiting for transfers between devices  155 us (22%)
  matrix products  81.2 us (12%)
  starting transfers between devices  39.2 us (6%)
  other arithmetic  13.8 us (2%)
    all_to_all x1, blocking collectives, local(): lax.all_to_all(outgoing, 'recv', split_axis=0, concat_axis=0, tiled=True)  197 us
    another operation x8, local copies, waits for them, and re-layouts, one_kernel(): jnp.stack(pieces, axis=2).reshape(per_kernel * BLOCK, lag_count * width)  130 us
    all_to_all x1, waiting for transfers between devices, local(): lax.all_to_all(outgoing, 'recv', split_axis=0, concat_axis=0, tiled=True)  92.2 us
    dot_general x8, matrix products, one_kernel(): jnp.einsum('mk,rk->mr', stacked_rows, kern, precision=lax.Precision.HIGHEST)  79.5 us
    ppermute x4, waiting for transfers between devices, local(): lax.ppermute(summed_all, 'src', [(dev, dev ^ hop) for dev in range(4)])  52.4 us
    all_to_all x1, starting transfers between devices, local(): lax.all_to_all(wanted.reshape(n_recv, peer_cap), 'recv', split_axis=0, co...  18.5 us
    gather x2, local copies, waits for them, and re-layouts, cut_window(): lax.dynamic_slice_in_dim(window, 2 * BLOCK - delay - (lag_count - 1), BLO...  17 us
    slice x8, local copies, waits for them, and re-layouts, one_kernel(): segs[:, lag_count - 1 - lag_idx:lag_count - 1 - lag_idx + BLOCK]  15.3 us
  transfers between devices with their start and end apart: 6, of which 6 were waited for; matrix products, arithmetic and copies ran while one was open for 1% of the time, Pallas kernels for 0%

profile of v1, /device:TPU:94, one launch (start us, length us, event | category | flops | bytes accessed | tf_op | source)
XLA Modules:
  0.0 683.3 jit_solution(4461931983708196237)
XLA Ops:
  2.7 18.5 %all-to-all-start = ((s32[128,1,1]{2,1,0:T(1,128)}), s32[128,1,1]{2,1,0:T(1,128)S(1)}, u32[]{:S(2)}, u32[]{:S(2)}) async-start(s32[128,1,1]{2,1,0:T(1,128)} %copy.163), calls=%async_computation | async-start | bytes 131072 | tf_op jit(solution)/shard_map/all_to_all | solution.py:59
  23.1 10.0 %all-to-all-done = s32[128,1,1]{2,1,0:T(1,128)S(1)} async-done(((s32[128,1,1]{2,1,0:T(1,128)}), s32[128,1,1]{2,1,0:T(1,128)S(1)}, u32[]{:S(2)}, u32[]{:S(2)}) %all-to-all-start) | async-done | bytes 544 | tf_op jit(solution)/shard_map/all_to_all | solution.py:59
  53.3 92.2 %all-to-all-done.1 = f32[128,1,32,128]{3,2,1,0:T(8,128)S(1)} async-done(((f32[128,1,32,128]{3,2,1,0:T(8,128)}), f32[128,1,32,128]{3,2,1,0:T(8,128)S(1)}, u32[]{:S(2)}, u32[]{:S(2)}) %all-to-all-start.1) | async-done | bytes 2097184 | tf_op jit(solution)/shard_map/all_to_all | solution.py:89
  160.0 117.6 %while.20 = (s32[]{:T(128)}, f32[4,768,128]{2,1,0:T(8,128)}, f32[4,24,47,128]{3,1,0,2:T(8,128)}, f32[4,128,2048]{2,1,0:T(8,128)}, s32[]{:T(128)}) while((s32[]{:T(128)}, f32[4,768,128]{2,1,0:T(8,128)}, f32[4,24,47,128]{3,1,0,2:T(8,128)}, f32[4,128,2048]{2,1,0:T(8,128)}, s32[]{:T(128)}) %tuple.88), condition=%wide.region_4.5_spmd, body=%wide.region_3.4_spmd.sunk | while | flops 2415919104 | bytes 35210304 | solution.py:94
  163.7 16.2 %stack.104 = f32[24,32,16,128]{3,2,1,0:T(8,128)} concatenate(f32[24,32,1,128]{3,2,1,0:T(1,128)} %bitcast.321, f32[24,32,1,128]{3,2,1,0:T(1,128)} %bitcast.320, f32[24,32,1,128]{3,2,1,0:T(1,128)} %bitcast.319, f32[24,32,1,128]{3,2,1,0:T(1,128)} %bitcast.318, f32[24,32,1,128]{3,2,1,0:T(1,128)} %bitcast.317, f32[24,32,1,128]{3,2,1,0:T(1,128)} %bitcast.316, ...), dimensions={2} | concatenate | bytes 12582912 | tf_op jit(solution)/shard_map/while/body/eval_jaxpr/stack | solution.py:78
  179.9 10.0 %fusion.113 = f32[4,768,128]{2,1,0:T(8,128)} fusion(f32[4,768,128]{2,1,0:T(8,128)} %get-tuple-element.267, s32[]{:T(128)} %get-tuple-element.266, f32[96,8,16,128]{3,2,1,0:T(8,128)} %bitcast.304, f32[4,128,2048]{2,1,0:T(8,128)} %get-tuple-element.274), kind=kOutput, calls=%fused_computation.10.clone.1 | convolution fusion | flops 2415919104 | bytes 7734272 | tf_op jit(solution)/shard_map/while/body/eval_jaxpr/mk,rk->mr/dot_general | solution.py:79
  193.0 16.2 %stack.104 = f32[24,32,16,128]{3,2,1,0:T(8,128)} concatenate(f32[24,32,1,128]{3,2,1,0:T(1,128)} %bitcast.321, f32[24,32,1,128]{3,2,1,0:T(1,128)} %bitcast.320, f32[24,32,1,128]{3,2,1,0:T(1,128)} %bitcast.319, f32[24,32,1,128]{3,2,1,0:T(1,128)} %bitcast.318, f32[24,32,1,128]{3,2,1,0:T(1,128)} %bitcast.317, f32[24,32,1,128]{3,2,1,0:T(1,128)} %bitcast.316, ...), dimensions={2} | concatenate | bytes 12582912 | tf_op jit(solution)/shard_map/while/body/eval_jaxpr/stack | solution.py:78
  222.2 16.2 %stack.104 = f32[24,32,16,128]{3,2,1,0:T(8,128)} concatenate(f32[24,32,1,128]{3,2,1,0:T(1,128)} %bitcast.321, f32[24,32,1,128]{3,2,1,0:T(1,128)} %bitcast.320, f32[24,32,1,128]{3,2,1,0:T(1,128)} %bitcast.319, f32[24,32,1,128]{3,2,1,0:T(1,128)} %bitcast.318, f32[24,32,1,128]{3,2,1,0:T(1,128)} %bitcast.317, f32[24,32,1,128]{3,2,1,0:T(1,128)} %bitcast.316, ...), dimensions={2} | concatenate | bytes 12582912 | tf_op jit(solution)/shard_map/while/body/eval_jaxpr/stack | solution.py:78
  238.4 9.9 %fusion.113 = f32[4,768,128]{2,1,0:T(8,128)} fusion(f32[4,768,128]{2,1,0:T(8,128)} %get-tuple-element.267, s32[]{:T(128)} %get-tuple-element.266, f32[96,8,16,128]{3,2,1,0:T(8,128)} %bitcast.304, f32[4,128,2048]{2,1,0:T(8,128)} %get-tuple-element.274), kind=kOutput, calls=%fused_computation.10.clone.1 | convolution fusion | flops 2415919104 | bytes 7734272 | tf_op jit(solution)/shard_map/while/body/eval_jaxpr/mk,rk->mr/dot_general | solution.py:79
  251.5 16.2 %stack.104 = f32[24,32,16,128]{3,2,1,0:T(8,128)} concatenate(f32[24,32,1,128]{3,2,1,0:T(1,128)} %bitcast.321, f32[24,32,1,128]{3,2,1,0:T(1,128)} %bitcast.320, f32[24,32,1,128]{3,2,1,0:T(1,128)} %bitcast.319, f32[24,32,1,128]{3,2,1,0:T(1,128)} %bitcast.318, f32[24,32,1,128]{3,2,1,0:T(1,128)} %bitcast.317, f32[24,32,1,128]{3,2,1,0:T(1,128)} %bitcast.316, ...), dimensions={2} | concatenate | bytes 12582912 | tf_op jit(solution)/shard_map/while/body/eval_jaxpr/stack | solution.py:78
  267.7 9.9 %fusion.113 = f32[4,768,128]{2,1,0:T(8,128)} fusion(f32[4,768,128]{2,1,0:T(8,128)} %get-tuple-element.267, s32[]{:T(128)} %get-tuple-element.266, f32[96,8,16,128]{3,2,1,0:T(8,128)} %bitcast.304, f32[4,128,2048]{2,1,0:T(8,128)} %get-tuple-element.274), kind=kOutput, calls=%fused_computation.10.clone.1 | convolution fusion | flops 2415919104 | bytes 7734272 | tf_op jit(solution)/shard_map/while/body/eval_jaxpr/mk,rk->mr/dot_general | solution.py:79
  282.8 13.0 %collective-permute-done = f32[32,32,128]{2,0,1:T(8,128)S(1)} collective-permute-done((f32[32,32,128]{2,0,1:T(8,128)S(1)}, f32[32,32,128]{2,0,1:T(8,128)S(1)}, u32[]{:S(2)}, u32[]{:S(2)}) %collective-permute-start) | collective-permute-done | bytes 524320 | tf_op jit(solution)/shard_map/ppermute | solution.py:101
  299.1 13.2 %collective-permute-done.1 = f32[32,32,128]{2,0,1:T(8,128)S(1)} collective-permute-done((f32[32,32,128]{2,0,1:T(8,128)S(1)}, f32[32,32,128]{2,0,1:T(8,128)S(1)}, u32[]{:S(2)}, u32[]{:S(2)}) %collective-permute-start.1) | collective-permute-done | bytes 524320 | tf_op jit(solution)/shard_map/ppermute | solution.py:101
  318.1 196.9 %all_to_all.25 = f32[128,1,64,128]{3,2,1,0:T(8,128)} all-to-all(f32[128,1,64,128]{3,2,1,0:T(8,128)S(1)} %fusion.24), channel_id=1, replica_groups=mesh['recv'=128,'src'=4] {'recv'}, dimensions={0} | all-to-all | bytes 8388608 | tf_op jit(solution)/shard_map/all_to_all | solution.py:89
  529.9 117.3 %while.21 = (s32[]{:T(128)}, f32[4,768,128]{2,1,0:T(8,128)}, f32[4,24,47,128]{3,1,0,2:T(8,128)}, f32[4,128,2048]{2,1,0:T(8,128)}, s32[]{:T(128)}) while((s32[]{:T(128)}, f32[4,768,128]{2,1,0:T(8,128)}, f32[4,24,47,128]{3,1,0,2:T(8,128)}, f32[4,128,2048]{2,1,0:T(8,128)}, s32[]{:T(128)}) %tuple.87), condition=%wide.region_6.7_spmd, body=%wide.region_5.6_spmd.sunk | while | flops 2415919104 | bytes 35210304 | solution.py:94
  533.2 16.2 %stack.105 = f32[24,32,16,128]{3,2,1,0:T(8,128)} concatenate(f32[24,32,1,128]{3,2,1,0:T(1,128)} %bitcast.337, f32[24,32,1,128]{3,2,1,0:T(1,128)} %bitcast.336, f32[24,32,1,128]{3,2,1,0:T(1,128)} %bitcast.335, f32[24,32,1,128]{3,2,1,0:T(1,128)} %bitcast.334, f32[24,32,1,128]{3,2,1,0:T(1,128)} %bitcast.333, f32[24,32,1,128]{3,2,1,0:T(1,128)} %bitcast.332, ...), dimensions={2} | concatenate | bytes 12582912 | tf_op jit(solution)/shard_map/while/body/eval_jaxpr/stack | solution.py:78
  549.4 10.0 %fusion.117 = f32[4,768,128]{2,1,0:T(8,128)} fusion(f32[4,768,128]{2,1,0:T(8,128)} %get-tuple-element.282, s32[]{:T(128)} %get-tuple-element.281, f32[96,8,16,128]{3,2,1,0:T(8,128)} %bitcast.305, f32[4,128,2048]{2,1,0:T(8,128)} %get-tuple-element.289), kind=kOutput, calls=%fused_computation.20.clone.1 | convolution fusion | flops 2415919104 | bytes 7734272 | tf_op jit(solution)/shard_map/while/body/eval_jaxpr/mk,rk->mr/dot_general | solution.py:79
  562.5 16.2 %stack.105 = f32[24,32,16,128]{3,2,1,0:T(8,128)} concatenate(f32[24,32,1,128]{3,2,1,0:T(1,128)} %bitcast.337, f32[24,32,1,128]{3,2,1,0:T(1,128)} %bitcast.336, f32[24,32,1,128]{3,2,1,0:T(1,128)} %bitcast.335, f32[24,32,1,128]{3,2,1,0:T(1,128)} %bitcast.334, f32[24,32,1,128]{3,2,1,0:T(1,128)} %bitcast.333, f32[24,32,1,128]{3,2,1,0:T(1,128)} %bitcast.332, ...), dimensions={2} | concatenate | bytes 12582912 | tf_op jit(solution)/shard_map/while/body/eval_jaxpr/stack | solution.py:78
  591.7 16.2 %stack.105 = f32[24,32,16,128]{3,2,1,0:T(8,128)} concatenate(f32[24,32,1,128]{3,2,1,0:T(1,128)} %bitcast.337, f32[24,32,1,128]{3,2,1,0:T(1,128)} %bitcast.336, f32[24,32,1,128]{3,2,1,0:T(1,128)} %bitcast.335, f32[24,32,1,128]{3,2,1,0:T(1,128)} %bitcast.334, f32[24,32,1,128]{3,2,1,0:T(1,128)} %bitcast.333, f32[24,32,1,128]{3,2,1,0:T(1,128)} %bitcast.332, ...), dimensions={2} | concatenate | bytes 12582912 | tf_op jit(solution)/shard_map/while/body/eval_jaxpr/stack | solution.py:78
  607.9 9.9 %fusion.117 = f32[4,768,128]{2,1,0:T(8,128)} fusion(f32[4,768,128]{2,1,0:T(8,128)} %get-tuple-element.282, s32[]{:T(128)} %get-tuple-element.281, f32[96,8,16,128]{3,2,1,0:T(8,128)} %bitcast.305, f32[4,128,2048]{2,1,0:T(8,128)} %get-tuple-element.289), kind=kOutput, calls=%fused_computation.20.clone.1 | convolution fusion | flops 2415919104 | bytes 7734272 | tf_op jit(solution)/shard_map/while/body/eval_jaxpr/mk,rk->mr/dot_general | solution.py:79
  621.0 16.2 %stack.105 = f32[24,32,16,128]{3,2,1,0:T(8,128)} concatenate(f32[24,32,1,128]{3,2,1,0:T(1,128)} %bitcast.337, f32[24,32,1,128]{3,2,1,0:T(1,128)} %bitcast.336, f32[24,32,1,128]{3,2,1,0:T(1,128)} %bitcast.335, f32[24,32,1,128]{3,2,1,0:T(1,128)} %bitcast.334, f32[24,32,1,128]{3,2,1,0:T(1,128)} %bitcast.333, f32[24,32,1,128]{3,2,1,0:T(1,128)} %bitcast.332, ...), dimensions={2} | concatenate | bytes 12582912 | tf_op jit(solution)/shard_map/while/body/eval_jaxpr/stack | solution.py:78
  637.2 9.9 %fusion.117 = f32[4,768,128]{2,1,0:T(8,128)} fusion(f32[4,768,128]{2,1,0:T(8,128)} %get-tuple-element.282, s32[]{:T(128)} %get-tuple-element.281, f32[96,8,16,128]{3,2,1,0:T(8,128)} %bitcast.305, f32[4,128,2048]{2,1,0:T(8,128)} %get-tuple-element.289), kind=kOutput, calls=%fused_computation.20.clone.1 | convolution fusion | flops 2415919104 | bytes 7734272 | tf_op jit(solution)/shard_map/while/body/eval_jaxpr/mk,rk->mr/dot_general | solution.py:79
  652.3 13.0 %collective-permute-done.2 = f32[32,32,128]{2,0,1:T(8,128)S(1)} collective-permute-done((f32[32,32,128]{2,0,1:T(8,128)S(1)}, f32[32,32,128]{2,0,1:T(8,128)S(1)}, u32[]{:S(2)}, u32[]{:S(2)}) %collective-permute-start.2) | collective-permute-done | bytes 524320 | tf_op jit(solution)/shard_map/ppermute | solution.py:101
  668.6 13.2 %collective-permute-done.3 = f32[32,32,128]{2,0,1:T(8,128)S(1)} collective-permute-done((f32[32,32,128]{2,0,1:T(8,128)S(1)}, f32[32,32,128]{2,0,1:T(8,128)S(1)}, u32[]{:S(2)}, u32[]{:S(2)}) %collective-permute-start.3) | collective-permute-done | bytes 524320 | tf_op jit(solution)/shard_map/ppermute | solution.py:101
  (129 shorter events, 122.0 us)
Async XLA Ops:
  2.7 30.4 %all-to-all-start = ((s32[128,1,1]{2,1,0:T(1,128)}), s32[128,1,1]{2,1,0:T(1,128)S(1)}, u32[]{:S(2)}, u32[]{:S(2)}) async-start(s32[128,1,1]{2,1,0:T(1,128)} %copy.163), calls=%async_computation | async-start | bytes 131072 | tf_op jit(solution)/shard_map/all_to_all | solution.py:59
  21.9 13.6 %copy-start.7 = (f32[8,128]{1,0:T(8,128)}, f32[8,128]{1,0:T(8,128)S(1)}, u32[]{:S(2)}) copy-start(f32[8,128]{1,0:T(8,128)S(1)} %get-tuple-element.139) | copy-start | bytes 12292
  21.9 13.6 %copy-start.10 = (f32[8,128]{1,0:T(8,128)}, f32[8,128]{1,0:T(8,128)S(1)}, u32[]{:S(2)}) copy-start(f32[8,128]{1,0:T(8,128)S(1)} %get-tuple-element.140) | copy-start | bytes 12292
  23.1 12.5 %copy-start = (f32[8,32,128]{2,0,1:T(8,128)}, f32[8,32,128]{2,0,1:T(8,128)S(1)}, u32[]{:S(2)}) copy-start(f32[8,32,128]{2,0,1:T(8,128)S(1)} %fusion.46) | copy-start | bytes 393220
  37.9 107.5 %all-to-all-start.1 = ((f32[128,1,32,128]{3,2,1,0:T(8,128)}), f32[128,1,32,128]{3,2,1,0:T(8,128)S(1)}, u32[]{:S(2)}, u32[]{:S(2)}) async-start(f32[128,1,32,128]{3,2,1,0:T(8,128)} %fusion.25), calls=%async_computation.1 | async-start | bytes 4194304 | tf_op jit(solution)/shard_map/all_to_all | solution.py:89
  47.1 6.2 copy-start.15
  53.3 95.7 %copy-start.16 = (pred[96]{0:T(512)(128)(4,1)}, pred[96]{0:T(512)(128)(4,1)S(1)}, u32[]{:S(2)}) copy-start(pred[96]{0:T(512)(128)(4,1)S(1)} %compare_and_fusion.1) | copy-start | bytes 292
  279.2 33.1 %copy-start.5 = (f32[8,128]{1,0:T(8,128)S(1)}, f32[8,128]{1,0:T(8,128)}, u32[]{:S(2)}) copy-start(f32[8,128]{1,0:T(8,128)} %param.14) | copy-start | bytes 12292
  279.2 33.0 %copy-start.8 = (f32[8,128]{1,0:T(8,128)S(1)}, f32[8,128]{1,0:T(8,128)}, u32[]{:S(2)}) copy-start(f32[8,128]{1,0:T(8,128)} %copy-done.7) | copy-start | bytes 12292
  279.2 33.0 %copy-start.11 = (f32[8,128]{1,0:T(8,128)S(1)}, f32[8,128]{1,0:T(8,128)}, u32[]{:S(2)}) copy-start(f32[8,128]{1,0:T(8,128)} %copy-done.10) | copy-start | bytes 12292
  279.2 33.0 %copy-start.20 = (f32[8,128]{1,0:T(8,128)S(1)}, f32[8,128]{1,0:T(8,128)}, u32[]{:S(2)}) copy-start(f32[8,128]{1,0:T(8,128)} %param.15) | copy-start | bytes 12292
  279.2 33.0 %copy-start.22 = (f32[8,128]{1,0:T(8,128)S(1)}, f32[8,128]{1,0:T(8,128)}, u32[]{:S(2)}) copy-start(f32[8,128]{1,0:T(8,128)} %param.13) | copy-start | bytes 12292
  279.2 33.5 %copy-start.1 = (f32[8,32,128]{2,0,1:T(8,128)S(1)}, f32[8,32,128]{2,0,1:T(8,128)}, u32[]{:S(2)}) copy-start(f32[8,32,128]{2,0,1:T(8,128)} %copy-done) | copy-start | bytes 393220
  280.1 15.7 %collective-permute-start = (f32[32,32,128]{2,0,1:T(8,128)S(1)}, f32[32,32,128]{2,0,1:T(8,128)S(1)}, u32[]{:S(2)}, u32[]{:S(2)}) collective-permute-start(f32[32,32,128]{2,0,1:T(8,128)S(1)} %fusion.29), channel_id=1, source_target_pairs={{0,1},{1,0},{2,3},{3,2},{4,5},{5,4},{6,7},{7,6},{8,9},{9,8},{10,11... | collective-permute-start | bytes 1572872 | tf_op jit(solution)/shard_map/ppermute | solution.py:101
  295.9 16.3 %collective-permute-start.1 = (f32[32,32,128]{2,0,1:T(8,128)S(1)}, f32[32,32,128]{2,0,1:T(8,128)S(1)}, u32[]{:S(2)}, u32[]{:S(2)}) collective-permute-start(f32[32,32,128]{2,0,1:T(8,128)S(1)} %add.344), channel_id=1, source_target_pairs={{0,2},{1,3},{2,0},{3,1},{4,6},{5,7},{6,4},{7,5},{8,10},{9,11},{10,... | collective-permute-start | bytes 1572872 | tf_op jit(solution)/shard_map/ppermute | solution.py:101
  648.7 33.1 %copy-start.6 = (f32[8,128]{1,0:T(8,128)S(1)}, f32[8,128]{1,0:T(8,128)}, u32[]{:S(2)}) copy-start(f32[8,128]{1,0:T(8,128)} %param.14) | copy-start | bytes 12292
  648.7 33.0 %copy-start.9 = (f32[8,128]{1,0:T(8,128)S(1)}, f32[8,128]{1,0:T(8,128)}, u32[]{:S(2)}) copy-start(f32[8,128]{1,0:T(8,128)} %copy-done.7) | copy-start | bytes 12292
  648.7 33.0 %copy-start.12 = (f32[8,128]{1,0:T(8,128)S(1)}, f32[8,128]{1,0:T(8,128)}, u32[]{:S(2)}) copy-start(f32[8,128]{1,0:T(8,128)} %copy-done.10) | copy-start | bytes 12292
  648.7 33.0 %copy-start.21 = (f32[8,128]{1,0:T(8,128)S(1)}, f32[8,128]{1,0:T(8,128)}, u32[]{:S(2)}) copy-start(f32[8,128]{1,0:T(8,128)} %param.15) | copy-start | bytes 12292
  648.7 33.0 %copy-start.23 = (f32[8,128]{1,0:T(8,128)S(1)}, f32[8,128]{1,0:T(8,128)}, u32[]{:S(2)}) copy-start(f32[8,128]{1,0:T(8,128)} %param.13) | copy-start | bytes 12292
  648.8 33.5 %copy-start.2 = (f32[8,32,128]{2,0,1:T(8,128)S(1)}, f32[8,32,128]{2,0,1:T(8,128)}, u32[]{:S(2)}) copy-start(f32[8,32,128]{2,0,1:T(8,128)} %copy-done) | copy-start | bytes 393220
  648.8 33.5 %copy-start.4 = (f32[8,32,128]{2,0,1:T(8,128)S(1)}, f32[8,32,128]{2,0,1:T(8,128)}, u32[]{:S(2)}) copy-start(f32[8,32,128]{2,0,1:T(8,128)} %copy-done.3) | copy-start | bytes 393220
  649.7 15.7 %collective-permute-start.2 = (f32[32,32,128]{2,0,1:T(8,128)S(1)}, f32[32,32,128]{2,0,1:T(8,128)S(1)}, u32[]{:S(2)}, u32[]{:S(2)}) collective-permute-start(f32[32,32,128]{2,0,1:T(8,128)S(1)} %fusion.26), channel_id=1, source_target_pairs={{0,1},{1,0},{2,3},{3,2},{4,5},{5,4},{6,7},{7,6},{8,9},{9,8},{10,11... | collective-permute-start | bytes 1572872 | tf_op jit(solution)/shard_map/ppermute | solution.py:101
  665.4 16.3 %collective-permute-start.3 = (f32[32,32,128]{2,0,1:T(8,128)S(1)}, f32[32,32,128]{2,0,1:T(8,128)S(1)}, u32[]{:S(2)}, u32[]{:S(2)}) collective-permute-start(f32[32,32,128]{2,0,1:T(8,128)S(1)} %add.363), channel_id=1, source_target_pairs={{0,2},{1,3},{2,0},{3,1},{4,6},{5,7},{6,4},{7,5},{8,10},{9,11},{10,... | collective-permute-start | bytes 1572872 | tf_op jit(solution)/shard_map/ppermute | solution.py:101
  (6 other events, 14.2 us)
